TPU v7x, 256 devices: a whole 4x4x8 slice. The times are simulated.
256 devices in a mesh: tensor: 8 (over z), dp: 32 (over x, y, core).
Axes of the slice: x: 4, y: 4, z: 8, core: 2. Of those that a mesh axis runs over, the one named last changes fastest.
Arguments:
- grads: bfloat16 [32, 4096, 2048], P('dp', 'tensor'), may hold values from -6 to 6
- errors: bfloat16 [32, 4096, 2048], P('dp', 'tensor'), may hold values from -4 to 4
- basis: float32 [2048, 64], replicated, may hold values from -6 to 6
- weight: float32 [4096, 2048], P(('tensor', 'dp')), may hold values from -6 to 6
- moment: float32 [4096, 2048], P(('tensor', 'dp')), may hold values from -0.125 to 0.125
- second: float32 [4096, 2048], P(('tensor', 'dp')), may hold values from 0.0002 to 0.05
Outputs:
- new_errors: bfloat16 [32, 4096, 2048], P('dp', 'tensor')
- basis_next: float32 [2048, 64], replicated
- weight_next: float32 [4096, 2048], P(('tensor', 'dp'))
- moment_next: float32 [4096, 2048], P(('tensor', 'dp'))
- second_next: float32 [4096, 2048], P(('tensor', 'dp'))
All inputs are finite; a program needn't handle non-finite values.
Results may differ from a plain program's by a relative error of at most 0.001.
Values sent between devices are 32-bit elements; how exact they have to be, the bound alone decides.
A program may use at most 64 MiB of HBM per device.

v0:
```python
import jax
import jax.numpy as jnp
from jax import lax
from jax.sharding import PartitionSpec as P

beta_first = 0.9
beta_second = 0.95
step_size = 0.1
adam_eps = 1e-08
corr_first = 1.0 - 0.9**10
corr_second = 1.0 - 0.95**10


def body(grads, errors, basis, weight, moment, second):
    highest = lax.Precision.HIGHEST
    merged = grads[0].astype(jnp.float32) + errors[0].astype(jnp.float32)
    partial_left = jnp.dot(merged, basis, precision=highest, preferred_element_type=jnp.float32)
    inner = (((0,), (0,)), ((), ()))
    columns = lax.psum(partial_left, "dp")
    local_gram = lax.dot_general(
        columns, columns, inner, precision=highest, preferred_element_type=jnp.float32
    )
    gram = lax.psum(local_gram, "tensor")
    factor = jnp.linalg.cholesky(gram)
    ortho = lax.linalg.triangular_solve(
        factor, columns, left_side=False, lower=True, transpose_a=True
    )
    partial_right = lax.dot_general(
        merged, ortho, inner, precision=highest, preferred_element_type=jnp.float32
    )
    basis_next = lax.psum(partial_right, ("tensor", "dp")) / lax.axis_size("dp")
    approx = lax.dot_general(
        ortho,
        basis_next,
        (((1,), (1,)), ((), ())),
        precision=highest,
        preferred_element_type=jnp.float32,
    )
    new_errors = (merged - approx).astype(jnp.bfloat16)[None]
    owned = weight.shape[0]
    update = lax.dynamic_slice_in_dim(approx, lax.axis_index("dp") * owned, owned, 0)
    moment_next = beta_first * moment + (1.0 - beta_first) * update
    second_next = beta_second * second + (1.0 - beta_second) * update * update
    weight_next = weight - step_size * (moment_next / corr_first) / (
        jnp.sqrt(second_next / corr_second) + adam_eps
    )
    return (new_errors, basis_next, weight_next, moment_next, second_next)


def solution(mesh):
    placed = (
        P("dp", "tensor", None),
        P("dp", "tensor", None),
        P(),
        P(("tensor", "dp"), None),
        P(("tensor", "dp"), None),
        P(("tensor", "dp"), None),
    )
    return jax.shard_map(
        body,
        mesh=mesh,
        in_specs=placed,
        out_specs=(
            P("dp", "tensor", None),
            P(),
            P(("tensor", "dp"), None),
            P(("tensor", "dp"), None),
            P(("tensor", "dp"), None),
        ),
        check_vma=False,
    )
```

profile of v0, /device:TPU:1, one launch (start us, length us, event | category | flops | bytes accessed | tf_op | source)
XLA Modules:
  0.0 442.3 jit_solution(17178736858494999480)
XLA Ops:
  7.2 0.0 copy-start
  7.2 0.0 copy-start.1
  7.2 0.0 all-reduce.3.cloned.1.call-start
  7.2 1.0 copy-done
  8.2 7.4 %fusion.2 = f32[512,64]{0,1:T(8,128)} fusion(f32[2048,64]{0,1:T(8,128)S(1)} %copy-done, bf16[1,512,2048]{2,1,0:T(8,128)(2,1)} %param.7, bf16[1,512,2048]{2,1,0:T(8,128)(2,1)} %param.6), kind=kOutput, calls=%fused_computation.3 | convolution fusion | flops 808452096 | bytes 4849664 | tf_op jit(solution)/shard_map/dot_general | solution.py:17
  15.6 0.0 all-reduce.3.cloned.1.call-update
  15.6 0.0 all-reduce.5.cloned.1.call-start
  15.6 113.8 %all-reduce.3.cloned.1.call-done = f32[512,64]{0,1:T(8,128)} async-done(((f32[512,64]{0,1:T(8,128)}), f32[512,64]{0,1:T(8,128)}) %all-reduce.3.cloned.1.call-update) | async-done | bytes 131088 | tf_op jit(solution)/shard_map/psum | solution.py:19
  129.4 1.2 fusion.12
  130.7 23.0 %psum.22 = f32[64,64]{0,1:T(8,128)S(1)} all-reduce(f32[64,64]{0,1:T(8,128)S(1)} %fusion.12), channel_id=1, replica_groups=mesh['tensor'=8,'dp'=32] {'tensor'}, use_global_device_ids=true, to_apply=%region_1.0 | all-reduce | flops 4096 | bytes 32768 | tf_op jit(solution)/shard_map/psum | solution.py:23
  153.7 0.1 copy.12
  153.8 5.8 %cholesky.16 = f32[64,64]{1,0:T(8,128)S(1)} custom-call(f32[64,64]{1,0:T(8,128)S(1)} %fusion.10), custom_call_target="Cholesky" | custom-call | tf_op jit(solution)/shard_map/jit(cholesky)/cholesky | solution.py:24
  159.7 0.6 compare_reduce_fusion
  160.3 0.7 fusion.7
  161.0 4.9 %custom-call.6 = f32[1,64,64]{1,2,0:T(8,128)S(1)} custom-call(f32[1,64,64]{2,1,0:T(8,128)S(1)} %fusion.7), custom_call_target="InvertDiagBlocksLowerTriangular" | custom-call | tf_op jit(solution)/shard_map/triangular_solve | solution.py:25
  165.9 1.2 fusion.8
  167.1 0.0 copy-done.1
  167.1 5.5 %fusion = f32[2048,64]{0,1:T(8,128)} fusion(f32[512,64]{0,1:T(8,128)S(1)} %fusion.8, bf16[1,512,2048]{2,1,0:T(8,128)(2,1)S(1)} %copy-done.1, bf16[1,512,2048]{2,1,0:T(8,128)(2,1)} %param.6), kind=kOutput, calls=%fused_computation.1 | convolution fusion | flops 808452096 | bytes 4849664 | tf_op jit(solution)/shard_map/dot_general | solution.py:28
  172.7 0.0 all-reduce.5.cloned.1.call-update
  172.7 254.6 %all-reduce.5.cloned.1.call-done = f32[2048,64]{0,1:T(8,128)} async-done(((f32[2048,64]{0,1:T(8,128)}), f32[2048,64]{0,1:T(8,128)}) %all-reduce.5.cloned.1.call-update) | async-done | bytes 524304 | tf_op jit(solution)/shard_map/psum | solution.py:31
  427.3 0.0 copy-start.2
  427.3 1.2 broadcast_multiply_fusion
  428.6 0.0 copy-start.3
  428.6 3.5 fusion.13
  432.1 0.0 copy-done.2
  432.1 0.0 copy-start.4
  432.1 0.0 copy-start.5
  432.1 0.0 copy-start.6
  432.1 2.5 fusion.5
  434.7 0.0 copy-done.3
  434.7 0.0 copy-done.4
  434.7 0.0 copy-done.5
  434.7 0.0 copy-done.6
  434.7 0.8 divide_subtract_fusion
  (2 shorter events, 0.0 us)
Async XLA Ops:
  7.2 1.0 copy-start
  7.2 159.9 %copy-start.1 = (bf16[1,512,2048]{2,1,0:T(8,128)(2,1)S(1)}, bf16[1,512,2048]{2,1,0:T(8,128)(2,1)}, u32[]{:S(2)}) copy-start(bf16[1,512,2048]{2,1,0:T(8,128)(2,1)} %param.7) | copy-start | bytes 6291460
  7.2 122.2 %all-reduce.3.cloned.1.call-start = ((), (), s32[]{:S(2)}) async-start(), calls=%async_computation | async-start | bytes 262144 | tf_op jit(solution)/shard_map/psum | solution.py:19
  15.6 411.7 %all-reduce.5.cloned.1.call-start = ((), (), s32[]{:S(2)}) async-start(), calls=%async_computation.1 | async-start | bytes 1048576 | tf_op jit(solution)/shard_map/psum | solution.py:31
  427.3 4.8 %copy-start.2 = (bf16[1,512,2048]{2,1,0:T(8,128)(2,1)S(1)}, bf16[1,512,2048]{2,1,0:T(8,128)(2,1)}, u32[]{:S(2)}) copy-start(bf16[1,512,2048]{2,1,0:T(8,128)(2,1)} %param.6) | copy-start | bytes 6291460
  428.6 6.1 %copy-start.3 = (f32[2048,64]{0,1:T(8,128)}, f32[2048,64]{0,1:T(8,128)S(1)}, u32[]{:S(2)}) copy-start(f32[2048,64]{0,1:T(8,128)S(1)} %broadcast_multiply_fusion) | copy-start | bytes 1572868
  432.1 2.6 copy-start.4
  432.1 2.6 copy-start.5
  432.1 2.6 copy-start.6
Sparse Core Ops, SparseCore 0:
  15.7 113.6 all-reduce.2
  172.8 254.4 all-reduce.4
where the time goes:
time: 443 us; the launch traced here: 442 us
  waiting for transfers between devices  368 us (83%)
  blocking collectives  23 us (5%)
  matrix products  18.9 us (4%)
  other arithmetic  16.6 us (4%)
  between operations  14.2 us (3%)
    psum x1, waiting for transfers between devices, body(): basis_next = lax.psum(partial_right, ('tensor', 'dp')) / lax.axis_size('dp')  255 us
    psum x1, waiting for transfers between devices, body(): columns = lax.psum(partial_left, 'dp')  114 us
    psum x1, blocking collectives, body(): gram = lax.psum(local_gram, 'tensor')  23 us
  transfers between devices with their start and end apart: 2, of which 2 were waited for; matrix products, arithmetic and copies ran while one was open for 0% of the time, Pallas kernels for 0%

commit v1 on v0

v1 whole, which is shorter than its diff:
```python
import jax
import jax.numpy as jnp
from jax import lax
from jax.experimental import pallas as pl
from jax.experimental.pallas import tpu as pltpu
from jax.sharding import PartitionSpec as P

beta_first = 0.9
beta_second = 0.95
step_size = 0.1
adam_eps = 1e-08
corr_first = 1.0 - 0.9**10
corr_second = 1.0 - 0.95**10

MESH = pl.DeviceIdType.MESH
VMEM = pltpu.VMEM
f32, bf16 = jnp.float32, jnp.bfloat16
D, RANK, HID, HALF = 2048, 64, 512, 256
NX, NY, NZ = 4, 4, 8
NN = (((1,), (0,)), ((), ()))
NT = (((1,), (1,)), ((), ()))
TN = (((0,), (0,)), ((), ()))
HIGH = lax.Precision.HIGHEST


def split3(v):
    hi = v.astype(bf16)
    rest = v - hi.astype(f32)
    mid = rest.astype(bf16)
    lo = (rest - mid.astype(f32)).astype(bf16)
    return hi, mid, lo


def split2(v):
    hi = v.astype(bf16)
    return hi, (v - hi.astype(f32)).astype(bf16)


def dot(a, b, dims=NN):
    return lax.dot_general(a, b, dims, preferred_element_type=f32)


def fold(v):
    return v[0:RANK] + v[RANK : 2 * RANK] + v[2 * RANK : 3 * RANK]


def eliminate(a, start, stop):
    rows = lax.broadcasted_iota(jnp.int32, (RANK, 2 * RANK), 0)
    lanes = lax.broadcasted_iota(jnp.int32, (RANK, 2 * RANK), 1)

    def step(k, a):
        row = jnp.sum(jnp.where(rows == k, a, 0.0), axis=0, keepdims=True)
        col = jnp.sum(jnp.where(lanes == k, a, 0.0), axis=1, keepdims=True)
        pivot = jnp.sum(jnp.where(lanes[0:1] == k, row, 0.0), axis=1, keepdims=True)
        root = lax.sqrt(pivot)
        row = row / root
        below = a - (col / root) * row
        return jnp.where(rows > k, below, jnp.where(rows == k, row, a))

    return lax.fori_loop(start, stop, step, a)


def exchange_kernel(
    g_hbm, e_hbm, b_hbm, bn_ref, op_ref,
    g, e, b, own_part, sib_part, one, two, c_t, r_all, r_sib, rbuf, zbuf, gram_send, gbuf, tb, aug,
    in_sem, core_s, core_r, one_s, one_r, two_s, two_r, rc_s, rc_r, xy_s, xy_r, z_s, z_r, gr_s, gr_r, ag_s, ag_r, fw_s, fw_r,
):
    t = lax.axis_index("tensor")
    d = lax.axis_index("dp")
    x, y, c = d // 8, (d // 2) % NY, d % 2
    oc = 1 - c
    chip = x * NY + y

    def dev(tt, xx, yy, cc):
        return (tt, (xx * NY + yy) * 2 + cc)

    sib = dev(t, x, y, oc)

    def plane(dx, dy):
        return (x + dx) % NX, (y + dy) % NY

    def send(src, dst, ss, rs, to):
        pltpu.make_async_remote_copy(
            src_ref=src, dst_ref=dst, send_sem=ss, recv_sem=rs, device_id=to, device_id_type=MESH
        ).start()

    def got(ref, rs):
        pltpu.make_async_remote_copy(
            src_ref=ref, dst_ref=ref, send_sem=core_s, recv_sem=rs, device_id=sib, device_id_type=MESH
        ).wait_recv()

    def sent(ref, ss):
        pltpu.make_async_remote_copy(
            src_ref=ref, dst_ref=ref, send_sem=ss, recv_sem=core_r, device_id=sib, device_id_type=MESH
        ).wait_send()

    b_in = pltpu.make_async_copy(b_hbm, b, in_sem.at[0])
    b_in.start()
    loads = []
    for i, half in enumerate((oc, c)):
        rows = pl.ds(pl.multiple_of(half * HALF, HALF), HALF)
        for j, (src, dst) in enumerate(((g_hbm, g), (e_hbm, e))):
            cp = pltpu.make_async_copy(src.at[0, rows], dst.at[rows], in_sem.at[1 + 2 * i + j])
            cp.start()
            loads.append(cp)

    barrier = pltpu.get_barrier_semaphore()

    def greet(to):
        pl.semaphore_signal(barrier, inc=1, device_id=to, device_id_type=MESH)

    greet(sib)
    near = ((2, 2), (2, 1), (2, 3), (1, 2), (3, 2), (1, 1), (1, 3), (3, 1), (3, 3), (2, 0), (0, 2), (1, 0), (3, 0), (0, 1), (0, 3))
    for dz in (4, 3, 5, 2, 6, 1, 7):
        greet(dev((t + dz) % NZ, x, y, c))
    for dx, dy in near:
        xx, yy = plane(dx, dy)
        greet(dev(t, xx, yy, c))
    for k in (2, 1, 3):
        greet(dev(t, (x + k) % NX, y, oc))
        greet(dev(t, x, (y + k) % NY, oc))

    b_in.wait()
    bs = jnp.concatenate(split3(b[...]), axis=0)

    def left(half, pair):
        rows = pl.ds(pl.multiple_of(half * HALF, HALF), HALF)
        pair[0].wait()
        acc = dot(bs, g[rows, :], NT)
        pair[1].wait()
        return fold(acc + dot(bs, e[rows, :], NT))

    own_part[...] = left(oc, loads[0:2])
    pl.semaphore_wait(barrier, 29)
    send(own_part, sib_part, core_s, core_r, sib)
    mine = left(c, loads[2:4])
    pos_one = jnp.where(c == 0, x, y)
    pos_two = jnp.where(c == 0, y, x)
    got(sib_part, core_r)
    one[pos_one] = mine + sib_part[...]
    for k in (2, 1, 3):
        to = dev(t, (x + k * oc) % NX, (y + k * c) % NY, c)
        send(one.at[pos_one], one.at[pos_one], one_s, one_r, to)
    got(one.at[pl.ds(0, 3)], one_r)
    slot = c * 4 + pos_two
    two[slot] = (one[0] + one[1]) + (one[2] + one[3])
    for k in (2, 1, 3):
        xx, yy = (x + k * c) % NX, (y + k * oc) % NY
        for cc in (c, oc):
            send(two.at[slot], two.at[slot], two_s, two_r, dev(t, xx, yy, cc))
    send(two.at[slot], two.at[slot], two_s, two_r, sib)
    got(two.at[pl.ds(0, 7)], two_r)
    for half in range(2):
        c_t[:, half * HALF : (half + 1) * HALF] = (two[4 * half] + two[4 * half + 1]) + (
            two[4 * half + 2] + two[4 * half + 3]
        )

    cs = jnp.concatenate(split3(c_t[...]), axis=0)
    for i, dx in enumerate((2, 1, 3, 0)):
        xx = (x + dx) % NX
        cols = pl.ds(pl.multiple_of(xx * 512, 512), 512)
        r = fold(dot(cs, g[:, cols]) + dot(cs, e[:, cols]))
        for yy in range(NY):
            for half in range(2):
                r_all[xx * NY + yy, half] = r[32 * half : 32 * half + 32, 128 * yy : 128 * yy + 128]
        four = pl.ds(xx * NY, NY)
        send(r_all.at[four, oc], r_sib.at[four], rc_s.at[i], rc_r.at[i], sib)

    gram = lax.dot_general(c_t[...], c_t[...], NT, precision=HIGH, preferred_element_type=f32)
    gbuf[t] = jnp.concatenate([gram[0:32], gram[32:64]], axis=1)
    for dz in (4, 3, 5, 2, 6, 1, 7):
        send(gbuf.at[t], gbuf.at[t], gr_s, gr_r, dev((t + dz) % NZ, x, y, c))

    for i, dx in enumerate((2, 1, 3, 0)):
        xx = (x + dx) % NX
        four = pl.ds(xx * NY, NY)
        got(r_sib.at[four], rc_r.at[i])
        for dy in (2, 1, 3, 0):
            yy = (y + dy) % NY
            n = xx * NY + yy
            summed = r_all[n, c] + r_sib[n]
            if dx == 0 and dy == 0:
                rbuf[n] = summed
            else:
                r_sib[n] = summed
                send(r_sib.at[n], rbuf.at[chip], xy_s, xy_r, dev(t, xx, yy, c))
    got(rbuf.at[pl.ds(0, 15)], xy_r)
    total = rbuf[0]
    for n in range(1, 16):
        total = total + rbuf[n]
    zbuf[t] = total
    for dz in (4, 3, 5, 2, 6, 1, 7):
        send(zbuf.at[t], zbuf.at[t], z_s, z_r, dev((t + dz) % NZ, x, y, c))

    got(gbuf.at[pl.ds(0, 7)], gr_r)
    packed = gbuf[0]
    for n in range(1, NZ):
        packed = packed + gbuf[n]
    rows = lax.broadcasted_iota(jnp.int32, (RANK, RANK), 0)
    lanes = lax.broadcasted_iota(jnp.int32, (RANK, RANK), 1)
    gram = jnp.concatenate([packed[:, 0:64], packed[:, 64:128]], axis=0)
    a = jnp.concatenate([gram, jnp.where(rows == lanes, 1.0, 0.0)], axis=1)
    aug[...] = eliminate(a, 0, 32)

    got(zbuf.at[pl.ds(0, 7)], z_r)
    total = zbuf[0]
    for n in range(1, NZ):
        total = total + zbuf[n]
    tb[chip, c] = total
    for dx, dy in near:
        xx, yy = plane(dx, dy)
        send(tb.at[chip, c], tb.at[chip, c], ag_s, ag_r, dev(t, xx, yy, c))

    inv = eliminate(aug[...], 32, 64)[:, RANK : 2 * RANK]
    o_t = lax.dot_general(inv, c_t[...], NN, precision=HIGH, preferred_element_type=f32)
    ortho = o_t.T
    o_hi, o_lo = split2(ortho)
    op_ref[0:HID, :] = jnp.concatenate([o_hi, o_hi, o_lo], axis=1)
    op_ref[HID : HID + 16, :] = op_ref[pl.ds(pl.multiple_of(d * 16, 16), 16), :]
    i_hi, i_lo = split2(inv * (1.0 / 32.0))
    inv_parts = jnp.concatenate([i_hi, i_hi, i_lo], axis=1)

    got(tb.at[pl.ds(0, 15), 0], ag_r)
    send(tb.at[:, c], tb.at[:, c], fw_s, fw_r, sib)
    got(tb.at[:, oc], fw_r)
    for n in range(0, 16, 2):
        blk = jnp.concatenate(
            [jnp.concatenate([tb[m, 0], tb[m, 1]], axis=0) for m in (n, n + 1)], axis=1
        )
        t_hi, t_lo = split2(blk)
        bn_ref[:, 128 * n : 128 * n + 256] = dot(inv_parts, jnp.concatenate([t_hi, t_lo, t_hi], axis=0))

    sent(own_part, core_s)
    sent(one.at[pl.ds(0, 3)], one_s)
    sent(two.at[pl.ds(0, 7)], two_s)
    for i in range(4):
        sent(r_sib.at[pl.ds(0, NY)], rc_s.at[i])
    sent(rbuf.at[pl.ds(0, 15)], xy_s)
    sent(zbuf.at[pl.ds(0, 7)], z_s)
    sent(gbuf.at[pl.ds(0, 7)], gr_s)
    sent(rbuf.at[pl.ds(0, 15)], ag_s)
    sent(rbuf, fw_s)


def exchange(g, e, b_t):
    any_ = pl.BlockSpec(memory_space=pl.ANY)
    vm = pl.BlockSpec(memory_space=VMEM)
    dma = pltpu.SemaphoreType.DMA
    return pl.pallas_call(
        exchange_kernel,
        name="exchange",
        out_shape=(
            jax.ShapeDtypeStruct((RANK, D), f32),
            jax.ShapeDtypeStruct((HID + 16, 3 * RANK), bf16),
        ),
        in_specs=[any_] * 3,
        out_specs=(vm, vm),
        scratch_shapes=[
            VMEM((HID, D), bf16),
            VMEM((HID, D), bf16),
            VMEM((RANK, D), f32),
            VMEM((RANK, HALF), f32),
            VMEM((RANK, HALF), f32),
            VMEM((4, RANK, HALF), f32),
            VMEM((8, RANK, HALF), f32),
            VMEM((RANK, HID), f32),
            VMEM((16, 2, 32, 128), f32),
            VMEM((16, 32, 128), f32),
            VMEM((16, 32, 128), f32),
            VMEM((NZ, 32, 128), f32),
            VMEM((32, 128), f32),
            VMEM((NZ, 32, 128), f32),
            VMEM((16, 2, 32, 128), f32),
            VMEM((RANK, 2 * RANK), f32),
            dma((5,)),
            dma, dma, dma, dma, dma, dma,
            dma((4,)), dma((4,)),
            dma, dma, dma, dma, dma, dma, dma, dma, dma, dma,
        ],
        compiler_params=pltpu.CompilerParams(
            collective_id=0, has_side_effects=True, vmem_limit_bytes=24 << 20
        ),
    )(g, e, b_t)


def apply_kernel(
    bn_ref, op_ref, g_ref, e_ref, w_ref, m_ref, s_ref, ne_hbm, bo_ref, wo_ref, mo_ref, so_ref, ne, sem
):
    op = op_ref[...]
    copies = []
    for j in range(8):
        cols = slice(256 * j, 256 * j + 256)
        bn = bn_ref[:, cols]
        bo_ref[:, cols] = bn
        hi, lo = split2(bn)
        approx = dot(op, jnp.concatenate([hi, lo, hi], axis=0))
        merged = g_ref[0, :, cols].astype(f32) + e_ref[0, :, cols].astype(f32)
        ne[:, cols] = (merged - approx[0:HID]).astype(bf16)
        cp = pltpu.make_async_copy(ne.at[:, cols], ne_hbm.at[0, :, cols], sem.at[j])
        cp.start()
        copies.append(cp)
        update = approx[HID : HID + 16]
        moment_next = beta_first * m_ref[:, cols] + (1.0 - beta_first) * update
        second_next = beta_second * s_ref[:, cols] + (1.0 - beta_second) * update * update
        mo_ref[:, cols] = moment_next
        so_ref[:, cols] = second_next
        wo_ref[:, cols] = w_ref[:, cols] - step_size * (moment_next / corr_first) / (
            jnp.sqrt(second_next / corr_second) + adam_eps
        )
    for cp in copies:
        cp.wait()


def apply(bn, op, g, e, w, m, s):
    vm = pl.BlockSpec(memory_space=VMEM)
    rows = jax.ShapeDtypeStruct(w.shape, f32)
    return pl.pallas_call(
        apply_kernel,
        name="apply",
        out_shape=(
            jax.ShapeDtypeStruct(g.shape, bf16),
            jax.ShapeDtypeStruct((RANK, D), f32),
            rows, rows, rows,
        ),
        in_specs=[vm] * 7,
        out_specs=(pl.BlockSpec(memory_space=pl.ANY), vm, vm, vm, vm),
        scratch_shapes=[VMEM((HID, D), bf16), pltpu.SemaphoreType.DMA((8,))],
        compiler_params=pltpu.CompilerParams(vmem_limit_bytes=24 << 20),
    )(bn, op, g, e, w, m, s)


def body(grads, errors, basis, weight, moment, second):
    bn, op = exchange(grads, errors, basis.T)
    new_errors, bo, w, m, s = apply(bn, op, grads, errors, weight, moment, second)
    return new_errors, bo.T, w, m, s


def solution(mesh):
    placed = (
        P("dp", "tensor", None),
        P("dp", "tensor", None),
        P(),
        P(("tensor", "dp"), None),
        P(("tensor", "dp"), None),
        P(("tensor", "dp"), None),
    )
    return jax.shard_map(
        body,
        mesh=mesh,
        in_specs=placed,
        out_specs=(
            P("dp", "tensor", None),
            P(),
            P(("tensor", "dp"), None),
            P(("tensor", "dp"), None),
            P(("tensor", "dp"), None),
        ),
        check_vma=False,
    )
```

time: 443 us -> 50.7 us (0.11)
  waiting for transfers between devices: 368 us -> 0 us
  Pallas kernels: 0 us -> 45.6 us
  blocking collectives: 23 us -> 0 us
  matrix products: 18.9 us -> 0 us
  other arithmetic: 16.6 us -> 0 us
  between operations: 14.2 us -> 0.68 us
    psum x2 -> x0, waiting for transfers between devices: 368 us -> none  [the longest x1 255 us: body(): basis_next = lax.psum(partial_right, ('tensor', 'dp')) / lax.axis_size('dp')]
    pallas_call x0 -> x2, Pallas kernels: none -> 45.6 us  [the longest x1 42.8 us: exchange(): pl.pallas_call(exchange_kernel, name='exchange', out_shape=(jax.ShapeDtyp...]
    psum x1 -> x0, blocking collectives: 23 us -> none  [body(): gram = lax.psum(local_gram, 'tensor')]
    dot_general x4 -> x0, matrix products: 17.6 us -> none  [the longest x1 7.36 us: body(): jnp.dot(merged, basis, precision=highest, preferred_element_type=jnp.floa...]
    another operation x5 -> x0, other arithmetic: 12.1 us -> none  [the longest x3 6.52 us: body(): factor = jnp.linalg.cholesky(gram)]
  transfers between devices with their start and end apart: 2 -> 0, of which waited for: 2 -> 0; matrix products, arithmetic and copies ran while one was open for 0% -> 0% of each run, Pallas kernels for 0% -> 0%
where the time goes in v1:
time: 50.7 us; the launch traced here: 50.5 us
  Pallas kernels  45.6 us (90%)
  local copies, waits for them, and re-layouts  4.23 us (8%)
  between operations  0.68 us (1%)
    pallas_call x1, Pallas kernels, exchange(): pl.pallas_call(exchange_kernel, name='exchange', out_shape=(jax.ShapeDtyp...  42.8 us
    unnamed x12, local copies, waits for them, and re-layouts  4.23 us
    pallas_call x1, Pallas kernels, apply(): pl.pallas_call(apply_kernel, name='apply', out_shape=(jax.ShapeDtypeStruc...  2.79 us

profile of v1, /device:TPU:1, one launch (start us, length us, event | category | flops | bytes accessed | tf_op | source)
XLA Modules:
  0.0 50.5 jit_solution(17055900977480207824)
XLA Ops:
  0.6 0.0 copy-start
  0.6 1.6 %copy-done = bf16[1,512,2048]{2,1,0:T(8,128)(2,1)S(1)} copy-done((bf16[1,512,2048]{2,1,0:T(8,128)(2,1)S(1)}, bf16[1,512,2048]{2,1,0:T(8,128)(2,1)}, u32[]{:S(2)}) %copy-start) | copy-done | bytes 2097176
  2.2 0.0 copy-start.1
  2.2 1.6 %copy-done.1 = bf16[1,512,2048]{2,1,0:T(8,128)(2,1)S(1)} copy-done((bf16[1,512,2048]{2,1,0:T(8,128)(2,1)S(1)}, bf16[1,512,2048]{2,1,0:T(8,128)(2,1)}, u32[]{:S(2)}) %copy-start.1) | copy-done | bytes 2097176
  3.8 0.0 copy-start.2
  3.8 1.0 %copy-done.2 = f32[2048,64]{0,1:T(8,128)S(1)} copy-done((f32[2048,64]{0,1:T(8,128)S(1)}, f32[2048,64]{0,1:T(8,128)}, u32[]{:S(2)}) %copy-start.2) | copy-done | bytes 524312
  4.9 0.0 copy-start.3
  4.9 0.0 copy-start.4
  4.9 0.0 copy-start.5
  4.9 42.8 %exchange.1 = (f32[64,2048]{1,0:T(8,128)S(1)}, bf16[528,192]{1,0:T(8,128)(2,1)S(1)}) custom-call(bf16[1,512,2048]{2,1,0:T(8,128)(2,1)S(1)} %copy-done, bf16[1,512,2048]{2,1,0:T(8,128)(2,1)S(1)} %copy-done.1, f32[64,2048]{1,0:T(8,128)S(1)} %bitcast.2), custom_call_target="tpu_custom_call" | custom-call | tf_op jit(solution)/shard_map/exchange/pallas_call | solution.py:249
  47.7 0.0 copy-done.3
  47.7 0.0 copy-done.4
  47.7 0.0 copy-done.5
  47.7 2.8 %apply.1 = (bf16[1,512,2048]{2,1,0:T(8,128)(2,1)}, f32[64,2048]{1,0:T(8,128)}, f32[16,2048]{1,0:T(8,128)}, f32[16,2048]{1,0:T(8,128)}, f32[16,2048]{1,0:T(8,128)}) custom-call(f32[64,2048]{1,0:T(8,128)S(1)} %get-tuple-element.12.bn_ref, bf16[528,192]{1,0:T(8,128)(2,1)S(1)} %get-tuple-element.13.op_ref, bf16[1,512,2048]{2,1,0:T(8,128)(2,1)S(1)} %copy-done, ...), custom_call_target="tpu_custom_call" | custom-call | tf_op jit(solution)/shard_map/apply/pallas_call | solution.py:317
Async XLA Ops:
  0.6 1.6 %copy-start = (bf16[1,512,2048]{2,1,0:T(8,128)(2,1)S(1)}, bf16[1,512,2048]{2,1,0:T(8,128)(2,1)}, u32[]{:S(2)}) copy-start(bf16[1,512,2048]{2,1,0:T(8,128)(2,1)} %g_ref.1) | copy-start | bytes 6291460
  2.2 1.6 %copy-start.1 = (bf16[1,512,2048]{2,1,0:T(8,128)(2,1)S(1)}, bf16[1,512,2048]{2,1,0:T(8,128)(2,1)}, u32[]{:S(2)}) copy-start(bf16[1,512,2048]{2,1,0:T(8,128)(2,1)} %e_ref.1) | copy-start | bytes 6291460
  3.8 1.0 %copy-start.2 = (f32[2048,64]{0,1:T(8,128)S(1)}, f32[2048,64]{0,1:T(8,128)}, u32[]{:S(2)}) copy-start(f32[2048,64]{0,1:T(8,128)} %param.8) | copy-start | bytes 1572868
  4.9 42.8 %copy-start.3 = (f32[16,2048]{1,0:T(8,128)S(1)}, f32[16,2048]{1,0:T(8,128)}, u32[]{:S(2)}) copy-start(f32[16,2048]{1,0:T(8,128)} %w_ref.1) | copy-start | bytes 393220
  4.9 42.8 %copy-start.4 = (f32[16,2048]{1,0:T(8,128)S(1)}, f32[16,2048]{1,0:T(8,128)}, u32[]{:S(2)}) copy-start(f32[16,2048]{1,0:T(8,128)} %m_ref.1) | copy-start | bytes 393220
  4.9 42.8 %copy-start.5 = (f32[16,2048]{1,0:T(8,128)S(1)}, f32[16,2048]{1,0:T(8,128)}, u32[]{:S(2)}) copy-start(f32[16,2048]{1,0:T(8,128)} %s_ref.1) | copy-start | bytes 393220

commit v2 on v1

v2 whole, which is shorter than its diff:
```python
import jax
import jax.numpy as jnp
from jax import lax
from jax.experimental import pallas as pl
from jax.experimental.pallas import tpu as pltpu
from jax.sharding import PartitionSpec as P

beta_first = 0.9
beta_second = 0.95
step_size = 0.1
adam_eps = 1e-08
corr_first = 1.0 - 0.9**10
corr_second = 1.0 - 0.95**10

MESH = pl.DeviceIdType.MESH
VMEM = pltpu.VMEM
f32, bf16 = jnp.float32, jnp.bfloat16
D, RANK, HID, HALF = 2048, 64, 512, 256
NX, NY, NZ = 4, 4, 8
NN = (((1,), (0,)), ((), ()))
NT = (((1,), (1,)), ((), ()))
TN = (((0,), (0,)), ((), ()))
HIGH = lax.Precision.HIGHEST


def split3(v):
    hi = v.astype(bf16)
    rest = v - hi.astype(f32)
    mid = rest.astype(bf16)
    lo = (rest - mid.astype(f32)).astype(bf16)
    return hi, mid, lo


def split2(v):
    hi = v.astype(bf16)
    return hi, (v - hi.astype(f32)).astype(bf16)


def dot(a, b, dims=NN):
    return lax.dot_general(a, b, dims, preferred_element_type=f32)


def fold(v):
    return v[0:RANK] + v[RANK : 2 * RANK] + v[2 * RANK : 3 * RANK]


def sub_row(v, k):
    return jnp.broadcast_to(v[k : k + 1, :], v.shape)


def inverse_factor(a):
    blocks = [a[8 * v : 8 * v + 8] for v in range(8)]
    sub = lax.broadcasted_iota(jnp.int32, (8, 2 * RANK), 0)
    lane = lax.broadcasted_iota(jnp.int32, (8, 2 * RANK), 1)
    for v in range(8):
        cols = {
            u: [jnp.broadcast_to(blocks[u][:, 8 * v + j : 8 * v + j + 1], (8, 2 * RANK)) for j in range(8)]
            for u in range(v, 8)
        }
        for k in range(8):
            over = 1.0 / sub_row(cols[v][k], k)
            later = [sub_row(cols[v][j], k) for j in range(k + 1, 8)]
            row = sub_row(blocks[v], k)
            for u in range(v, 8):
                times = cols[u][k] * over
                if u == v:
                    times = jnp.where(sub > k, times, 0.0)
                for j in range(k + 1, 8):
                    cols[u][j] = cols[u][j] - times * later[j - k - 1]
                blocks[u] = blocks[u] - times * row
    out = []
    for v in range(8):
        pivots = jnp.sum(jnp.where(lane == sub + 8 * v, blocks[v], 0.0), axis=1, keepdims=True)
        out.append(blocks[v] / lax.sqrt(pivots))
    return jnp.concatenate(out, axis=0)[:, RANK:]


FAR = ((2, 2), (2, 1), (2, 3), (1, 2), (3, 2), (1, 1), (1, 3), (3, 1), (3, 3), (2, 0), (0, 2), (1, 0), (3, 0), (0, 1), (0, 3))
ZFAR = (4, 3, 5, 2, 6, 1, 7)


def exchange_kernel(
    g_hbm, e_hbm, b_hbm, tb, op_ref, ip_ref, g, e,
    b, p_send, p_recv, c_buf, c_t, r_all, r_sib, rbuf, zbuf, gbuf,
    in_sem, p_s, p_r, c_s, c_r, rc_s, rc_r, xy_s, xy_r, z_s, z_r, gr_s, gr_r, ag_s, ag_r, fw_s, fw_r,
):
    t = lax.axis_index("tensor")
    d = lax.axis_index("dp")
    x, y, c = d // 8, (d // 2) % NY, d % 2
    oc = 1 - c
    chip = x * NY + y

    def dev(tt, xx, yy, cc):
        return (tt, (xx * NY + yy) * 2 + cc)

    sib = dev(t, x, y, oc)

    def send(src, dst, ss, rs, to):
        pltpu.make_async_remote_copy(
            src_ref=src, dst_ref=dst, send_sem=ss, recv_sem=rs, device_id=to, device_id_type=MESH
        ).start()

    def got(ref, rs):
        pltpu.make_async_remote_copy(
            src_ref=ref, dst_ref=ref, send_sem=p_s, recv_sem=rs, device_id=sib, device_id_type=MESH
        ).wait_recv()

    def sent(ref, ss):
        pltpu.make_async_remote_copy(
            src_ref=ref, dst_ref=ref, send_sem=ss, recv_sem=p_r, device_id=sib, device_id_type=MESH
        ).wait_send()

    barrier = pltpu.get_barrier_semaphore()

    def greet(to):
        pl.semaphore_signal(barrier, inc=1, device_id=to, device_id_type=MESH)

    b_in = pltpu.make_async_copy(b_hbm, b, in_sem.at[0])
    b_in.start()
    x_far = (x + 2) % NX
    x_near = x + 1 - 2 * (x % 2)
    x_mid = x_far + 1 - 2 * (x_far % 2)
    halves = (x_far // 2, x // 2)
    loads = []
    for i, half in enumerate(halves):
        for j, (src, dst) in enumerate(((g_hbm, g), (e_hbm, e))):
            for k in range(2):
                rows = pl.ds(pl.multiple_of(half * HALF + 128 * k, 128), 128)
                cp = pltpu.make_async_copy(src.at[0, rows], dst.at[rows], in_sem.at[1 + 4 * i + 2 * j + k])
                cp.start()
                loads.append(cp)
        if i == 0:
            for dz in ZFAR:
                greet(dev((t + dz) % NZ, x, y, c))
            for dx, dy in FAR:
                for cc in (c, oc):
                    greet(dev(t, (x + dx) % NX, (y + dy) % NY, cc))
            greet(sib)

    b_in.wait()
    bs = jnp.concatenate(split3(b[...]), axis=0)
    for i, half in enumerate(halves):
        rows = pl.ds(pl.multiple_of(half * HALF, HALF), HALF)
        loads[4 * i].wait()
        loads[4 * i + 1].wait()
        acc = dot(bs, g[rows, :], NT)
        loads[4 * i + 2].wait()
        loads[4 * i + 3].wait()
        part = fold(acc + dot(bs, e[rows, :], NT))
        for j in range(2):
            for k in range(8):
                p_send[16 * half + 8 * j + k] = part[8 * k : 8 * k + 8, 128 * j : 128 * j + 128]
        if i == 0:
            pl.semaphore_wait(barrier, 38)
        for xx in ((x_far, x_mid), (x_near, x))[i]:
            for dy in (2, 1, 3, 0):
                yy = (y + dy) % NY
                for cc in (oc, c):
                    n = (xx * NY + yy) * 2 + cc
                    if xx is x and dy == 0 and cc is c:
                        p_recv[n] = p_send[n]
                    else:
                        send(p_send.at[n], p_recv.at[d], p_s, p_r, dev(t, xx, yy, cc))
    got(p_recv.at[pl.ds(0, 31)], p_r)
    total = p_recv[0]
    for n in range(1, 32):
        total = total + p_recv[n]
    c_buf[d] = total
    for dx, dy in FAR + ((0, 0),):
        for cc in (oc, c):
            if not (dx == 0 and dy == 0 and cc is c):
                send(c_buf.at[d], c_buf.at[d], c_s, c_r, dev(t, (x + dx) % NX, (y + dy) % NY, cc))
    got(c_buf.at[pl.ds(0, 31)], c_r)
    for j in range(4):
        c_t[:, 128 * j : 128 * j + 128] = c_buf[8 * j : 8 * j + 8].reshape(RANK, 128)

    cs = jnp.concatenate(split3(c_t[...]), axis=0)

    def right(i, dx):
        xx = (x + dx) % NX
        cols = pl.ds(pl.multiple_of(xx * 512, 512), 512)
        r = fold(dot(cs, g[:, cols]) + dot(cs, e[:, cols]))
        for yy in range(NY):
            for half in range(2):
                r_all[xx * NY + yy, half] = r[32 * half : 32 * half + 32, 128 * yy : 128 * yy + 128]
        four = pl.ds(xx * NY, NY)
        send(r_all.at[four, oc], r_sib.at[four], rc_s.at[i], rc_r.at[i], sib)

    def scatter(i, dx):
        xx = (x + dx) % NX
        four = pl.ds(xx * NY, NY)
        got(r_sib.at[four], rc_r.at[i])
        if dx:
            r_sib[four] = r_all[four, c] + r_sib[four]
        else:
            for dy in (2, 1, 3, 0):
                n = xx * NY + (y + dy) % NY
                summed = r_all[n, c] + r_sib[n]
                if dy:
                    r_sib[n] = summed
                else:
                    rbuf[n] = summed
        for dy in (2, 1, 3, 0):
            yy = (y + dy) % NY
            if dx or dy:
                send(r_sib.at[xx * NY + yy], rbuf.at[chip], xy_s, xy_r, dev(t, xx, yy, c))

    right(0, 2)
    right(1, 1)
    right(2, 3)
    scatter(0, 2)
    right(3, 0)
    scatter(1, 1)
    scatter(2, 3)
    scatter(3, 0)
    gram = lax.dot_general(c_t[...], c_t[...], NT, precision=HIGH, preferred_element_type=f32)
    gbuf[t] = jnp.concatenate([gram[0:32], gram[32:64]], axis=1)
    for dz in ZFAR:
        send(gbuf.at[t], gbuf.at[t], gr_s, gr_r, dev((t + dz) % NZ, x, y, c))

    got(rbuf.at[pl.ds(0, 15)], xy_r)
    total = rbuf[0]
    for n in range(1, 16):
        total = total + rbuf[n]
    zbuf[t] = total
    for dz in ZFAR:
        send(zbuf.at[t], zbuf.at[t], z_s, z_r, dev((t + dz) % NZ, x, y, c))

    got(gbuf.at[pl.ds(0, 7)], gr_r)
    packed = gbuf[0]
    for n in range(1, NZ):
        packed = packed + gbuf[n]
    rows = lax.broadcasted_iota(jnp.int32, (RANK, RANK), 0)
    lanes = lax.broadcasted_iota(jnp.int32, (RANK, RANK), 1)
    gram = jnp.concatenate([packed[:, 0:64], packed[:, 64:128]], axis=0)
    a = jnp.concatenate([gram, jnp.where(rows == lanes, 1.0, 0.0)], axis=1)
    inv = inverse_factor(a)
    o_t = lax.dot_general(inv, c_t[...], NN, precision=HIGH, preferred_element_type=f32)
    o_hi, o_lo = split2(o_t.T)
    op_ref[0:HID, :] = jnp.concatenate([o_hi, o_hi, o_lo], axis=1)
    op_ref[HID : HID + 16, :] = op_ref[pl.ds(pl.multiple_of(d * 16, 16), 16), :]
    i_hi, i_lo = split2(inv * (1.0 / 32.0))
    ip_ref[...] = jnp.concatenate([i_hi, i_hi, i_lo], axis=1)

    got(zbuf.at[pl.ds(0, 7)], z_r)
    total = zbuf[0]
    for n in range(1, NZ):
        total = total + zbuf[n]
    tb[chip, c] = total
    for dx, dy in FAR:
        send(tb.at[chip, c], tb.at[chip, c], ag_s, ag_r.at[chip], dev(t, (x + dx) % NX, (y + dy) % NY, c))
    send(tb.at[chip, c], tb.at[chip, c], fw_s, fw_r.at[chip], sib)

    for dx, dy in FAR:
        n = ((x + dx) % NX) * NY + (y + dy) % NY
        got(tb.at[n, c], ag_r.at[n])
        send(tb.at[n, c], tb.at[n, c], fw_s, fw_r.at[n], sib)
    for dx, dy in ((0, 0),) + FAR:
        n = ((x + dx) % NX) * NY + (y + dy) % NY
        got(tb.at[n, oc], fw_r.at[n])

    sent(p_recv.at[pl.ds(0, 31)], p_s)
    sent(p_recv.at[pl.ds(0, 31)], c_s)
    for i in range(4):
        sent(r_sib.at[pl.ds(0, NY)], rc_s.at[i])
    sent(rbuf.at[pl.ds(0, 15)], xy_s)
    sent(zbuf.at[pl.ds(0, 7)], z_s)
    sent(gbuf.at[pl.ds(0, 7)], gr_s)
    sent(rbuf.at[pl.ds(0, 15)], ag_s)
    sent(rbuf, fw_s)


def exchange(g, e, b_t):
    hbm = pl.BlockSpec(memory_space=pltpu.HBM)
    vm = pl.BlockSpec(memory_space=VMEM)
    dma = pltpu.SemaphoreType.DMA
    return pl.pallas_call(
        exchange_kernel,
        name="exchange",
        out_shape=(
            jax.ShapeDtypeStruct((16, 2, 32, 128), f32),
            jax.ShapeDtypeStruct((HID + 16, 3 * RANK), bf16),
            jax.ShapeDtypeStruct((RANK, 3 * RANK), bf16),
            jax.ShapeDtypeStruct((HID, D), bf16),
            jax.ShapeDtypeStruct((HID, D), bf16),
        ),
        in_specs=[hbm] * 3,
        out_specs=(vm,) * 5,
        scratch_shapes=[
            VMEM((RANK, D), f32),
            VMEM((32, 8, 128), f32),
            VMEM((32, 8, 128), f32),
            VMEM((32, 8, 128), f32),
            VMEM((RANK, HID), f32),
            VMEM((16, 2, 32, 128), f32),
            VMEM((16, 32, 128), f32),
            VMEM((16, 32, 128), f32),
            VMEM((NZ, 32, 128), f32),
            VMEM((NZ, 32, 128), f32),
            dma((9,)),
            dma, dma, dma, dma,
            dma((4,)), dma((4,)),
            dma, dma, dma, dma, dma, dma,
            dma, dma((16,)), dma, dma((16,)),
        ],
        compiler_params=pltpu.CompilerParams(
            collective_id=0, has_side_effects=True, vmem_limit_bytes=24 << 20
        ),
    )(*(pltpu.with_memory_space_constraint(v, pltpu.HBM) for v in (g, e, b_t)))


def apply_kernel(
    tb_ref, op_ref, ip_ref, g_ref, e_ref, w_ref, m_ref, s_ref, ne_hbm, bo_hbm, wo_hbm, mo_hbm, so_hbm,
    bn, ne, wo, mo, so, sem,
):
    op, ip = op_ref[...], ip_ref[...]
    copies = []

    def out(src, dst):
        cp = pltpu.make_async_copy(src, dst, sem.at[len(copies)])
        cp.start()
        copies.append(cp)

    for j in range(8):
        cols = slice(256 * j, 256 * j + 256)
        block = jnp.concatenate([tb_ref[n].reshape(RANK, 128) for n in (2 * j, 2 * j + 1)], axis=1)
        hi, lo = split2(block)
        right = dot(ip, jnp.concatenate([hi, lo, hi], axis=0))
        bn[:, cols] = right
        hi, lo = split2(right)
        approx = dot(op, jnp.concatenate([hi, lo, hi], axis=0))
        merged = g_ref[:, cols].astype(f32) + e_ref[:, cols].astype(f32)
        ne[:, cols] = (merged - approx[0:HID]).astype(bf16)
        out(ne.at[:, cols], ne_hbm.at[0, :, cols])
        update = approx[HID : HID + 16]
        moment_next = beta_first * m_ref[:, cols] + (1.0 - beta_first) * update
        second_next = beta_second * s_ref[:, cols] + (1.0 - beta_second) * update * update
        mo[:, cols] = moment_next
        so[:, cols] = second_next
        wo[:, cols] = w_ref[:, cols] - step_size * (moment_next / corr_first) / (
            jnp.sqrt(second_next / corr_second) + adam_eps
        )
    out(bn, bo_hbm)
    out(mo, mo_hbm)
    out(so, so_hbm)
    out(wo, wo_hbm)
    for cp in copies:
        cp.wait()


def apply(tb, op, ip, g, e, w, m, s):
    vm = pl.BlockSpec(memory_space=VMEM)
    rows = jax.ShapeDtypeStruct(w.shape, f32)
    return pl.pallas_call(
        apply_kernel,
        name="apply",
        out_shape=(
            jax.ShapeDtypeStruct((1, HID, D), bf16),
            jax.ShapeDtypeStruct((RANK, D), f32),
            rows, rows, rows,
        ),
        in_specs=[vm] * 8,
        out_specs=(pl.BlockSpec(memory_space=pltpu.HBM),) * 5,
        scratch_shapes=[VMEM((RANK, D), f32), VMEM((HID, D), bf16)] + [VMEM(w.shape, f32)] * 3 + [pltpu.SemaphoreType.DMA((12,))],
        compiler_params=pltpu.CompilerParams(vmem_limit_bytes=24 << 20),
    )(tb, op, ip, g, e, w, m, s)


def body(grads, errors, basis, weight, moment, second):
    tb, op, ip, g, e = exchange(grads, errors, basis.T)
    new_errors, bo, w, m, s = apply(tb, op, ip, g, e, weight, moment, second)
    return new_errors, bo.T, w, m, s


def solution(mesh):
    placed = (
        P("dp", "tensor", None),
        P("dp", "tensor", None),
        P(),
        P(("tensor", "dp"), None),
        P(("tensor", "dp"), None),
        P(("tensor", "dp"), None),
    )
    return jax.shard_map(
        body,
        mesh=mesh,
        in_specs=placed,
        out_specs=(
            P("dp", "tensor", None),
            P(),
            P(("tensor", "dp"), None),
            P(("tensor", "dp"), None),
            P(("tensor", "dp"), None),
        ),
        check_vma=False,
    )
```

time: 50.7 us -> 45 us (0.89)
  local copies, waits for them, and re-layouts: 4.23 us -> 0.01 us
  Pallas kernels: 45.6 us -> 44.2 us
    unnamed x12 -> x6, local copies, waits for them, and re-layouts: 4.23 us -> 0.01 us
    pallas_call x1, Pallas kernels: 42.8 us -> 41.4 us  [exchange(): pl.pallas_call(exchange_kernel, name='exchange', out_shape=(jax.ShapeDtyp...]
where the time goes in v2:
time: 45 us; the launch traced here: 44.9 us
  Pallas kernels  44.2 us (98%)
  between operations  0.69 us (2%)
    pallas_call x1, Pallas kernels, exchange(): pl.pallas_call(exchange_kernel, name='exchange', out_shape=(jax.ShapeDtyp...  41.4 us
    pallas_call x1, Pallas kernels, apply(): pl.pallas_call(apply_kernel, name='apply', out_shape=(jax.ShapeDtypeStruc...  2.72 us

profile of v2, /device:TPU:1, one launch (start us, length us, event | category | flops | bytes accessed | tf_op | source)
XLA Modules:
  0.0 44.9 jit_solution(9360775731167636814)
XLA Ops:
  0.6 0.0 copy-start
  0.6 0.0 copy-start.1
  0.7 0.0 copy-start.2
  0.7 41.4 %exchange.1 = (f32[16,2,32,128]{3,2,1,0:T(8,128)S(1)}, bf16[528,192]{1,0:T(8,128)(2,1)S(1)}, bf16[64,192]{1,0:T(8,128)(2,1)S(1)}, bf16[512,2048]{1,0:T(8,128)(2,1)S(1)}, bf16[512,2048]{1,0:T(8,128)(2,1)S(1)}) custom-call(bf16[1,512,2048]{2,1,0:T(8,128)(2,1)} %g_hbm.1, bf16[1,512,2048]{2,1,0:T(8,128)(2,1)} %e_hbm.1, f32[64,2048]{1,0:T(8,128)} %bitcast.2), custom_call_target="tpu_custom_call" | custom-call | tf_op jit(solution)/shard_map/exchange/pallas_call | solution.py:277
  42.1 0.0 copy-done
  42.1 0.0 copy-done.1
  42.1 0.0 copy-done.2
  42.1 2.7 %apply.1 = (bf16[1,512,2048]{2,1,0:T(8,128)(2,1)}, f32[64,2048]{1,0:T(8,128)}, f32[16,2048]{1,0:T(8,128)}, f32[16,2048]{1,0:T(8,128)}, f32[16,2048]{1,0:T(8,128)}) custom-call(f32[16,2,32,128]{3,2,1,0:T(8,128)S(1)} %get-tuple-element.15.tb_ref, bf16[528,192]{1,0:T(8,128)(2,1)S(1)} %get-tuple-element.16.op_ref, bf16[64,192]{1,0:T(8,128)(2,1)S(1)} %get-tuple-element.17.ip_ref, ...), custom_call_target="tpu_custom_call" | custom-call | tf_op jit(solution)/shard_map/apply/pallas_call | solution.py:354
Async XLA Ops:
  0.6 41.5 %copy-start = (f32[16,2048]{1,0:T(8,128)S(1)}, f32[16,2048]{1,0:T(8,128)}, u32[]{:S(2)}) copy-start(f32[16,2048]{1,0:T(8,128)} %w_ref.1) | copy-start | bytes 393220
  0.6 41.5 %copy-start.1 = (f32[16,2048]{1,0:T(8,128)S(1)}, f32[16,2048]{1,0:T(8,128)}, u32[]{:S(2)}) copy-start(f32[16,2048]{1,0:T(8,128)} %m_ref.1) | copy-start | bytes 393220
  0.7 41.5 %copy-start.2 = (f32[16,2048]{1,0:T(8,128)S(1)}, f32[16,2048]{1,0:T(8,128)}, u32[]{:S(2)}) copy-start(f32[16,2048]{1,0:T(8,128)} %s_ref.1) | copy-start | bytes 393220

commit v3 on v2

--- a/solution.py
+++ b/solution.py
@@ -15,7 +15,7 @@
 MESH = pl.DeviceIdType.MESH
 VMEM = pltpu.VMEM
 f32, bf16 = jnp.float32, jnp.bfloat16
-D, RANK, HID, HALF = 2048, 64, 512, 256
+D, RANK, HID, HALF, WIDE = 2048, 64, 512, 256, 1024
 NX, NY, NZ = 4, 4, 8
 NN = (((1,), (0,)), ((), ()))
 NT = (((1,), (1,)), ((), ()))
@@ -81,8 +81,8 @@
 
 def exchange_kernel(
     g_hbm, e_hbm, b_hbm, tb, op_ref, ip_ref, g, e,
-    b, p_send, p_recv, c_buf, c_t, r_all, r_sib, rbuf, zbuf, gbuf,
-    in_sem, p_s, p_r, c_s, c_r, rc_s, rc_r, xy_s, xy_r, z_s, z_r, gr_s, gr_r, ag_s, ag_r, fw_s, fw_r,
+    b, p_send, p_recv, c_buf, c_t, m_send, m_recv, s_hi, s_lo, r_all, rbuf, zbuf, gbuf,
+    in_sem, p_s, p_r, c_s, c_r, ms_s, ms_r, xy_s, xy_r, z_s, z_r, gr_s, gr_r, ag_s, ag_r, fw_s, fw_r,
 ):
     t = lax.axis_index("tensor")
     d = lax.axis_index("dp")
@@ -161,6 +161,12 @@
                         p_recv[n] = p_send[n]
                     else:
                         send(p_send.at[n], p_recv.at[d], p_s, p_r, dev(t, xx, yy, cc))
+    theirs = pl.ds(pl.multiple_of(oc * WIDE, WIDE), WIDE)
+    ours = pl.ds(pl.multiple_of(c * WIDE, WIDE), WIDE)
+    for k in range(4):
+        rows = pl.ds(128 * k, 128)
+        m_send[rows, :] = g[rows, theirs].astype(f32) + e[rows, theirs].astype(f32)
+        send(m_send.at[rows], m_recv.at[rows], ms_s.at[k], ms_r.at[k], sib)
     got(p_recv.at[pl.ds(0, 31)], p_r)
     total = p_recv[0]
     for n in range(1, 32):
@@ -170,49 +176,31 @@
         for cc in (oc, c):
             if not (dx == 0 and dy == 0 and cc is c):
                 send(c_buf.at[d], c_buf.at[d], c_s, c_r, dev(t, (x + dx) % NX, (y + dy) % NY, cc))
+    for k in range(4):
+        rows = pl.ds(128 * k, 128)
+        got(m_recv.at[rows], ms_r.at[k])
+        pair = (g[rows, ours].astype(f32) + e[rows, ours].astype(f32)) + m_recv[rows, :]
+        s_hi[rows, :], s_lo[rows, :] = split2(pair)
     got(c_buf.at[pl.ds(0, 31)], c_r)
     for j in range(4):
         c_t[:, 128 * j : 128 * j + 128] = c_buf[8 * j : 8 * j + 8].reshape(RANK, 128)
 
     cs = jnp.concatenate(split3(c_t[...]), axis=0)
 
-    def right(i, dx):
+    for dx in (2, 0, 1, 3):
         xx = (x + dx) % NX
-        cols = pl.ds(pl.multiple_of(xx * 512, 512), 512)
-        r = fold(dot(cs, g[:, cols]) + dot(cs, e[:, cols]))
+        cols = pl.ds(pl.multiple_of(xx * 256, 256), 256)
+        r = fold(dot(cs, s_hi[:, cols]) + dot(cs, s_lo[:, cols]))
         for yy in range(NY):
-            for half in range(2):
-                r_all[xx * NY + yy, half] = r[32 * half : 32 * half + 32, 128 * yy : 128 * yy + 128]
-        four = pl.ds(xx * NY, NY)
-        send(r_all.at[four, oc], r_sib.at[four], rc_s.at[i], rc_r.at[i], sib)
-
-    def scatter(i, dx):
-        xx = (x + dx) % NX
-        four = pl.ds(xx * NY, NY)
-        got(r_sib.at[four], rc_r.at[i])
-        if dx:
-            r_sib[four] = r_all[four, c] + r_sib[four]
-        else:
-            for dy in (2, 1, 3, 0):
-                n = xx * NY + (y + dy) % NY
-                summed = r_all[n, c] + r_sib[n]
-                if dy:
-                    r_sib[n] = summed
-                else:
-                    rbuf[n] = summed
+            half, blk = yy % 2, yy // 2
+            r_all[xx * NY + yy] = r[32 * half : 32 * half + 32, 128 * blk : 128 * blk + 128]
         for dy in (2, 1, 3, 0):
             yy = (y + dy) % NY
+            n = xx * NY + yy
             if dx or dy:
-                send(r_sib.at[xx * NY + yy], rbuf.at[chip], xy_s, xy_r, dev(t, xx, yy, c))
-
-    right(0, 2)
-    right(1, 1)
-    right(2, 3)
-    scatter(0, 2)
-    right(3, 0)
-    scatter(1, 1)
-    scatter(2, 3)
-    scatter(3, 0)
+                send(r_all.at[n], rbuf.at[chip], xy_s, xy_r, dev(t, xx, yy, c))
+            else:
+                rbuf[chip] = r_all[chip]
     gram = lax.dot_general(c_t[...], c_t[...], NT, precision=HIGH, preferred_element_type=f32)
     gbuf[t] = jnp.concatenate([gram[0:32], gram[32:64]], axis=1)
     for dz in ZFAR:
@@ -261,8 +249,8 @@
 
     sent(p_recv.at[pl.ds(0, 31)], p_s)
     sent(p_recv.at[pl.ds(0, 31)], c_s)
-    for i in range(4):
-        sent(r_sib.at[pl.ds(0, NY)], rc_s.at[i])
+    for k in range(4):
+        sent(m_recv.at[pl.ds(128 * k, 128)], ms_s.at[k])
     sent(rbuf.at[pl.ds(0, 15)], xy_s)
     sent(zbuf.at[pl.ds(0, 7)], z_s)
     sent(gbuf.at[pl.ds(0, 7)], gr_s)
@@ -292,7 +280,10 @@
             VMEM((32, 8, 128), f32),
             VMEM((32, 8, 128), f32),
             VMEM((RANK, HID), f32),
-            VMEM((16, 2, 32, 128), f32),
+            VMEM((HID, WIDE), f32),
+            VMEM((HID, WIDE), f32),
+            VMEM((HID, WIDE), bf16),
+            VMEM((HID, WIDE), bf16),
             VMEM((16, 32, 128), f32),
             VMEM((16, 32, 128), f32),
             VMEM((NZ, 32, 128), f32),
@@ -321,14 +312,19 @@
         cp.start()
         copies.append(cp)
 
+    parts = []
+    for j in range(8):
+        half, k = j // 4, 4 * (j % 4)
+        pieces = [tb_ref[n : n + 2, half].reshape(RANK, 128) for n in (k, k + 2)]
+        hi, lo = split2(jnp.concatenate(pieces, axis=1))
+        right = dot(ip, jnp.concatenate([hi, lo, hi], axis=0))
+        bn[:, 256 * j : 256 * j + 256] = right
+        hi, lo = split2(right)
+        parts.append(jnp.concatenate([hi, lo, hi], axis=0))
+    out(bn, bo_hbm)
     for j in range(8):
         cols = slice(256 * j, 256 * j + 256)
-        block = jnp.concatenate([tb_ref[n].reshape(RANK, 128) for n in (2 * j, 2 * j + 1)], axis=1)
-        hi, lo = split2(block)
-        right = dot(ip, jnp.concatenate([hi, lo, hi], axis=0))
-        bn[:, cols] = right
-        hi, lo = split2(right)
-        approx = dot(op, jnp.concatenate([hi, lo, hi], axis=0))
+        approx = dot(op, parts[j])
         merged = g_ref[:, cols].astype(f32) + e_ref[:, cols].astype(f32)
         ne[:, cols] = (merged - approx[0:HID]).astype(bf16)
         out(ne.at[:, cols], ne_hbm.at[0, :, cols])
@@ -340,7 +336,6 @@
         wo[:, cols] = w_ref[:, cols] - step_size * (moment_next / corr_first) / (
             jnp.sqrt(second_next / corr_second) + adam_eps
         )
-    out(bn, bo_hbm)
     out(mo, mo_hbm)
     out(so, so_hbm)
     out(wo, wo_hbm)

time: 45 us -> 42.7 us (0.949)
  Pallas kernels: 44.2 us -> 41.9 us
    pallas_call x1, Pallas kernels: 41.4 us -> 39.6 us  [exchange(): pl.pallas_call(exchange_kernel, name='exchange', out_shape=(jax.ShapeDtyp...]
where the time goes in v3:
time: 42.7 us; the launch traced here: 42.6 us
  Pallas kernels  41.9 us (98%)
  between operations  0.69 us (2%)
    pallas_call x1, Pallas kernels, exchange(): pl.pallas_call(exchange_kernel, name='exchange', out_shape=(jax.ShapeDtyp...  39.6 us
    pallas_call x1, Pallas kernels, apply(): pl.pallas_call(apply_kernel, name='apply', out_shape=(jax.ShapeDtypeStruc...  2.31 us

profile of v3, /device:TPU:1, one launch (start us, length us, event | category | flops | bytes accessed | tf_op | source)
XLA Modules:
  0.0 42.6 jit_solution(5166446653232852910)
XLA Ops:
  0.6 0.0 copy-start
  0.6 0.0 copy-start.1
  0.7 0.0 copy-start.2
  0.7 39.6 %exchange.1 = (f32[16,2,32,128]{3,2,1,0:T(8,128)S(1)}, bf16[528,192]{1,0:T(8,128)(2,1)S(1)}, bf16[64,192]{1,0:T(8,128)(2,1)S(1)}, bf16[512,2048]{1,0:T(8,128)(2,1)S(1)}, bf16[512,2048]{1,0:T(8,128)(2,1)S(1)}) custom-call(bf16[1,512,2048]{2,1,0:T(8,128)(2,1)} %g_hbm.1, bf16[1,512,2048]{2,1,0:T(8,128)(2,1)} %e_hbm.1, f32[64,2048]{1,0:T(8,128)} %bitcast.2), custom_call_target="tpu_custom_call" | custom-call | tf_op jit(solution)/shard_map/exchange/pallas_call | solution.py:265
  40.2 0.0 copy-done
  40.3 0.0 copy-done.1
  40.3 0.0 copy-done.2
  40.3 2.3 %apply.1 = (bf16[1,512,2048]{2,1,0:T(8,128)(2,1)}, f32[64,2048]{1,0:T(8,128)}, f32[16,2048]{1,0:T(8,128)}, f32[16,2048]{1,0:T(8,128)}, f32[16,2048]{1,0:T(8,128)}) custom-call(f32[16,2,32,128]{3,2,1,0:T(8,128)S(1)} %get-tuple-element.15.tb_ref, bf16[528,192]{1,0:T(8,128)(2,1)S(1)} %get-tuple-element.16.op_ref, bf16[64,192]{1,0:T(8,128)(2,1)S(1)} %get-tuple-element.17.ip_ref, ...), custom_call_target="tpu_custom_call" | custom-call | tf_op jit(solution)/shard_map/apply/pallas_call | solution.py:349
Async XLA Ops:
  0.6 39.6 %copy-start = (f32[16,2048]{1,0:T(8,128)S(1)}, f32[16,2048]{1,0:T(8,128)}, u32[]{:S(2)}) copy-start(f32[16,2048]{1,0:T(8,128)} %w_ref.1) | copy-start | bytes 393220
  0.6 39.6 %copy-start.1 = (f32[16,2048]{1,0:T(8,128)S(1)}, f32[16,2048]{1,0:T(8,128)}, u32[]{:S(2)}) copy-start(f32[16,2048]{1,0:T(8,128)} %m_ref.1) | copy-start | bytes 393220
  0.7 39.6 %copy-start.2 = (f32[16,2048]{1,0:T(8,128)S(1)}, f32[16,2048]{1,0:T(8,128)}, u32[]{:S(2)}) copy-start(f32[16,2048]{1,0:T(8,128)} %s_ref.1) | copy-start | bytes 393220

commit v4 on v3

--- a/solution.py
+++ b/solution.py
@@ -75,12 +75,24 @@
     return jnp.concatenate(out, axis=0)[:, RANK:]
 
 
+def blocks_of(tb, ip, core):
+    rights, parts = [], []
+    for j in range(4):
+        pieces = [tb[n : n + 2, core].reshape(RANK, 128) for n in (4 * j, 4 * j + 2)]
+        hi, lo = split2(jnp.concatenate(pieces, axis=1))
+        right = dot(ip, jnp.concatenate([hi, lo, hi], axis=0))
+        hi, lo = split2(right)
+        rights.append(right)
+        parts.append(jnp.concatenate([hi, lo, hi], axis=0))
+    return rights, parts
+
+
 FAR = ((2, 2), (2, 1), (2, 3), (1, 2), (3, 2), (1, 1), (1, 3), (3, 1), (3, 3), (2, 0), (0, 2), (1, 0), (3, 0), (0, 1), (0, 3))
 ZFAR = (4, 3, 5, 2, 6, 1, 7)
 
 
 def exchange_kernel(
-    g_hbm, e_hbm, b_hbm, tb, op_ref, ip_ref, g, e,
+    g_hbm, e_hbm, b_hbm, tb, op_ref, ip_ref, g, e, bn_ref, ne_ref, up_ref,
     b, p_send, p_recv, c_buf, c_t, m_send, m_recv, s_hi, s_lo, r_all, rbuf, zbuf, gbuf,
     in_sem, p_s, p_r, c_s, c_r, ms_s, ms_r, xy_s, xy_r, z_s, z_r, gr_s, gr_r, ag_s, ag_r, fw_s, fw_r,
 ):
@@ -243,6 +255,14 @@
         n = ((x + dx) % NX) * NY + (y + dy) % NY
         got(tb.at[n, c], ag_r.at[n])
         send(tb.at[n, c], tb.at[n, c], fw_s, fw_r.at[n], sib)
+    rights, parts = blocks_of(tb, ip_ref[...], c)
+    for j in range(4):
+        here = slice(256 * j, 256 * j + 256)
+        cols = pl.ds(pl.multiple_of(c * WIDE + 256 * j, 256), 256)
+        bn_ref[:, here] = rights[j]
+        approx = dot(op_ref[...], parts[j])
+        ne_ref[:, here] = (g[:, cols].astype(f32) + e[:, cols].astype(f32) - approx[0:HID]).astype(bf16)
+        up_ref[:, here] = approx[HID : HID + 16]
     for dx, dy in ((0, 0),) + FAR:
         n = ((x + dx) % NX) * NY + (y + dy) % NY
         got(tb.at[n, oc], fw_r.at[n])
@@ -271,9 +291,12 @@
             jax.ShapeDtypeStruct((RANK, 3 * RANK), bf16),
             jax.ShapeDtypeStruct((HID, D), bf16),
             jax.ShapeDtypeStruct((HID, D), bf16),
+            jax.ShapeDtypeStruct((RANK, WIDE), f32),
+            jax.ShapeDtypeStruct((HID, WIDE), bf16),
+            jax.ShapeDtypeStruct((16, WIDE), f32),
         ),
         in_specs=[hbm] * 3,
-        out_specs=(vm,) * 5,
+        out_specs=(vm,) * 8,
         scratch_shapes=[
             VMEM((RANK, D), f32),
             VMEM((32, 8, 128), f32),
@@ -301,10 +324,11 @@
 
 
 def apply_kernel(
-    tb_ref, op_ref, ip_ref, g_ref, e_ref, w_ref, m_ref, s_ref, ne_hbm, bo_hbm, wo_hbm, mo_hbm, so_hbm,
-    bn, ne, wo, mo, so, sem,
+    tb_ref, op_ref, ip_ref, g_ref, e_ref, bn_ref, ne_ref, up_ref, w_ref, m_ref, s_ref,
+    ne_hbm, bo_hbm, wo_hbm, mo_hbm, so_hbm, bn, ne, wo, mo, so, sem,
 ):
-    op, ip = op_ref[...], ip_ref[...]
+    c = lax.axis_index("dp") % 2
+    oc = 1 - c
     copies = []
 
     def out(src, dst):
@@ -312,23 +336,10 @@
         cp.start()
         copies.append(cp)
 
-    parts = []
-    for j in range(8):
-        half, k = j // 4, 4 * (j % 4)
-        pieces = [tb_ref[n : n + 2, half].reshape(RANK, 128) for n in (k, k + 2)]
-        hi, lo = split2(jnp.concatenate(pieces, axis=1))
-        right = dot(ip, jnp.concatenate([hi, lo, hi], axis=0))
-        bn[:, 256 * j : 256 * j + 256] = right
-        hi, lo = split2(right)
-        parts.append(jnp.concatenate([hi, lo, hi], axis=0))
-    out(bn, bo_hbm)
-    for j in range(8):
-        cols = slice(256 * j, 256 * j + 256)
-        approx = dot(op, parts[j])
-        merged = g_ref[:, cols].astype(f32) + e_ref[:, cols].astype(f32)
-        ne[:, cols] = (merged - approx[0:HID]).astype(bf16)
-        out(ne.at[:, cols], ne_hbm.at[0, :, cols])
-        update = approx[HID : HID + 16]
+    def span(half, start, size):
+        return pl.ds(pl.multiple_of(half * WIDE + start, size), size)
+
+    def adam(cols, update):
         moment_next = beta_first * m_ref[:, cols] + (1.0 - beta_first) * update
         second_next = beta_second * s_ref[:, cols] + (1.0 - beta_second) * update * update
         mo[:, cols] = moment_next
@@ -336,6 +347,24 @@
         wo[:, cols] = w_ref[:, cols] - step_size * (moment_next / corr_first) / (
             jnp.sqrt(second_next / corr_second) + adam_eps
         )
+
+    for j in range(2):
+        here = pl.ds(512 * j, 512)
+        out(ne_ref.at[:, here], ne_hbm.at[0, :, span(c, 512 * j, 512)])
+    out(bn_ref, bo_hbm.at[:, span(c, 0, WIDE)])
+    rights, parts = blocks_of(tb_ref, ip_ref[...], oc)
+    for j in range(4):
+        bn[:, 256 * j : 256 * j + 256] = rights[j]
+    out(bn, bo_hbm.at[:, span(oc, 0, WIDE)])
+    op = op_ref[...]
+    for j in range(4):
+        here = slice(256 * j, 256 * j + 256)
+        cols = span(oc, 256 * j, 256)
+        approx = dot(op, parts[j])
+        ne[:, here] = (g_ref[:, cols].astype(f32) + e_ref[:, cols].astype(f32) - approx[0:HID]).astype(bf16)
+        out(ne.at[:, here], ne_hbm.at[0, :, cols])
+        adam(cols, approx[HID : HID + 16])
+        adam(span(c, 256 * j, 256), up_ref[:, here])
     out(mo, mo_hbm)
     out(so, so_hbm)
     out(wo, wo_hbm)
@@ -343,7 +372,7 @@
         cp.wait()
 
 
-def apply(tb, op, ip, g, e, w, m, s):
+def apply(tb, op, ip, g, e, bn, ne, up, w, m, s):
     vm = pl.BlockSpec(memory_space=VMEM)
     rows = jax.ShapeDtypeStruct(w.shape, f32)
     return pl.pallas_call(
@@ -354,16 +383,16 @@
             jax.ShapeDtypeStruct((RANK, D), f32),
             rows, rows, rows,
         ),
-        in_specs=[vm] * 8,
+        in_specs=[vm] * 11,
         out_specs=(pl.BlockSpec(memory_space=pltpu.HBM),) * 5,
-        scratch_shapes=[VMEM((RANK, D), f32), VMEM((HID, D), bf16)] + [VMEM(w.shape, f32)] * 3 + [pltpu.SemaphoreType.DMA((12,))],
+        scratch_shapes=[VMEM((RANK, WIDE), f32), VMEM((HID, WIDE), bf16)] + [VMEM(w.shape, f32)] * 3 + [pltpu.SemaphoreType.DMA((12,))],
         compiler_params=pltpu.CompilerParams(vmem_limit_bytes=24 << 20),
-    )(tb, op, ip, g, e, w, m, s)
+    )(tb, op, ip, g, e, bn, ne, up, w, m, s)
 
 
 def body(grads, errors, basis, weight, moment, second):
-    tb, op, ip, g, e = exchange(grads, errors, basis.T)
-    new_errors, bo, w, m, s = apply(tb, op, ip, g, e, weight, moment, second)
+    parts = exchange(grads, errors, basis.T)
+    new_errors, bo, w, m, s = apply(*parts, weight, moment, second)
     return new_errors, bo.T, w, m, s
 
 

time: 42.7 us -> 42.1 us (0.986)
  Pallas kernels: 41.9 us -> 41.4 us
    pallas_call x1, Pallas kernels: 2.31 us -> 1.78 us  [apply(): pl.pallas_call(apply_kernel, name='apply', out_shape=(jax.ShapeDtypeStruc...]
where the time goes in v4:
time: 42.1 us
  Pallas kernels  41.4 us (98%)
  between operations  0.69 us (2%)
    pallas_call x1, Pallas kernels, exchange(): pl.pallas_call(exchange_kernel, name='exchange', out_shape=(jax.ShapeDtyp...  39.6 us
    pallas_call x1, Pallas kernels, apply(): pl.pallas_call(apply_kernel, name='apply', out_shape=(jax.ShapeDtypeStruc...  1.78 us

profile of v4, /device:TPU:1, one launch (start us, length us, event | category | flops | bytes accessed | tf_op | source)
XLA Modules:
  0.0 42.1 jit_solution(11765676031020288205)
XLA Ops:
  0.6 0.0 copy-start
  0.6 0.0 copy-start.1
  0.7 0.0 copy-start.2
  0.7 39.6 %exchange.1 = (f32[16,2,32,128]{3,2,1,0:T(8,128)S(1)}, bf16[528,192]{1,0:T(8,128)(2,1)S(1)}, bf16[64,192]{1,0:T(8,128)(2,1)S(1)}, bf16[512,2048]{1,0:T(8,128)(2,...) custom-call(bf16[1,512,2048]{2,1,0:T(8,128)(2,1)} %g_hbm.1, ...), custom_call_target="tpu_custom_call" | custom-call | tf_op jit(solution)/shard_map/exchange/pallas_call | solution.py:285
  40.2 0.0 copy-done
  40.3 0.0 copy-done.1
  40.3 0.0 copy-done.2
  40.3 1.8 %apply.1 = (bf16[1,512,2048]{2,1,0:T(8,128)(2,1)}, f32[64,2048]{1,0:T(8,128)}, f32[16,2048]{1,0:T(8,128)}, f32[16,2048]{1,0:T(8,128)}, f32[16,2048]{1,0:T(8,128)}) custom-call(f32[16,2,32,128]{3,2,1,0:T(8,128)S(1)} %get-tuple-element.18.tb_ref, bf16[528,192]{1,0:T(8,128)(2,1)S(1)} %get-tuple-element.19.op_ref, bf16[64,192]{1,0:T(8,128)(2,1)S(1)} %get-tuple-element.20.ip_ref, ...), custom_call_target="tpu_custom_call" | custom-call | tf_op jit(solution)/shard_map/apply/pallas_call | solution.py:378
Async XLA Ops:
  0.6 39.6 %copy-start = (f32[16,2048]{1,0:T(8,128)S(1)}, f32[16,2048]{1,0:T(8,128)}, u32[]{:S(2)}) copy-start(f32[16,2048]{1,0:T(8,128)} %w_ref.1) | copy-start | bytes 393220
  0.6 39.6 %copy-start.1 = (f32[16,2048]{1,0:T(8,128)S(1)}, f32[16,2048]{1,0:T(8,128)}, u32[]{:S(2)}) copy-start(f32[16,2048]{1,0:T(8,128)} %m_ref.1) | copy-start | bytes 393220
  0.7 39.6 %copy-start.2 = (f32[16,2048]{1,0:T(8,128)S(1)}, f32[16,2048]{1,0:T(8,128)}, u32[]{:S(2)}) copy-start(f32[16,2048]{1,0:T(8,128)} %s_ref.1) | copy-start | bytes 393220

commit v5 on v4

--- a/solution.py
+++ b/solution.py
@@ -127,8 +127,11 @@
     def greet(to):
         pl.semaphore_signal(barrier, inc=1, device_id=to, device_id_type=MESH)
 
-    b_in = pltpu.make_async_copy(b_hbm, b, in_sem.at[0])
-    b_in.start()
+    b_in = []
+    for k in range(4):
+        some = pl.ds(16 * k, 16)
+        b_in.append(pltpu.make_async_copy(b_hbm.at[some], b.at[some], in_sem.at[8 + k]))
+        b_in[k].start()
     x_far = (x + 2) % NX
     x_near = x + 1 - 2 * (x % 2)
     x_mid = x_far + 1 - 2 * (x_far % 2)
@@ -138,7 +141,7 @@
         for j, (src, dst) in enumerate(((g_hbm, g), (e_hbm, e))):
             for k in range(2):
                 rows = pl.ds(pl.multiple_of(half * HALF + 128 * k, 128), 128)
-                cp = pltpu.make_async_copy(src.at[0, rows], dst.at[rows], in_sem.at[1 + 4 * i + 2 * j + k])
+                cp = pltpu.make_async_copy(src.at[0, rows], dst.at[rows], in_sem.at[4 * i + 2 * j + k])
                 cp.start()
                 loads.append(cp)
         if i == 0:
@@ -149,7 +152,8 @@
                     greet(dev(t, (x + dx) % NX, (y + dy) % NY, cc))
             greet(sib)
 
-    b_in.wait()
+    for cp in b_in:
+        cp.wait()
     bs = jnp.concatenate(split3(b[...]), axis=0)
     for i, half in enumerate(halves):
         rows = pl.ds(pl.multiple_of(half * HALF, HALF), HALF)
@@ -311,7 +315,7 @@
             VMEM((16, 32, 128), f32),
             VMEM((NZ, 32, 128), f32),
             VMEM((NZ, 32, 128), f32),
-            dma((9,)),
+            dma((12,)),
             dma, dma, dma, dma,
             dma((4,)), dma((4,)),
             dma, dma, dma, dma, dma, dma,

time: 42.1 us -> 42.2 us (level)
  no operation moved by 1% of the time
where the time goes in v5:
time: 42.2 us; the launch traced here: 42.1 us
  Pallas kernels  41.4 us (98%)
  between operations  0.69 us (2%)
    pallas_call x1, Pallas kernels, exchange(): pl.pallas_call(exchange_kernel, name='exchange', out_shape=(jax.ShapeDtyp...  39.7 us
    pallas_call x1, Pallas kernels, apply(): pl.pallas_call(apply_kernel, name='apply', out_shape=(jax.ShapeDtypeStruc...  1.78 us

profile of v5, /device:TPU:1, one launch (start us, length us, event | category | flops | bytes accessed | tf_op | source)
XLA Modules:
  0.0 42.1 jit_solution(5002472780380992984)
XLA Ops:
  0.6 0.0 copy-start
  0.6 0.0 copy-start.1
  0.7 0.0 copy-start.2
  0.7 39.7 %exchange.1 = (f32[16,2,32,128]{3,2,1,0:T(8,128)S(1)}, bf16[528,192]{1,0:T(8,128)(2,1)S(1)}, bf16[64,192]{1,0:T(8,128)(2,1)S(1)}, bf16[512,2048]{1,0:T(8,128)(2,...) custom-call(bf16[1,512,2048]{2,1,0:T(8,128)(2,1)} %g_hbm.1, ...), custom_call_target="tpu_custom_call" | custom-call | tf_op jit(solution)/shard_map/exchange/pallas_call | solution.py:289
  40.3 0.0 copy-done
  40.3 0.0 copy-done.1
  40.3 0.0 copy-done.2
  40.4 1.8 %apply.1 = (bf16[1,512,2048]{2,1,0:T(8,128)(2,1)}, f32[64,2048]{1,0:T(8,128)}, f32[16,2048]{1,0:T(8,128)}, f32[16,2048]{1,0:T(8,128)}, f32[16,2048]{1,0:T(8,128)}) custom-call(f32[16,2,32,128]{3,2,1,0:T(8,128)S(1)} %get-tuple-element.18.tb_ref, bf16[528,192]{1,0:T(8,128)(2,1)S(1)} %get-tuple-element.19.op_ref, bf16[64,192]{1,0:T(8,128)(2,1)S(1)} %get-tuple-element.20.ip_ref, ...), custom_call_target="tpu_custom_call" | custom-call | tf_op jit(solution)/shard_map/apply/pallas_call | solution.py:382
Async XLA Ops:
  0.6 39.7 %copy-start = (f32[16,2048]{1,0:T(8,128)S(1)}, f32[16,2048]{1,0:T(8,128)}, u32[]{:S(2)}) copy-start(f32[16,2048]{1,0:T(8,128)} %w_ref.1) | copy-start | bytes 393220
  0.6 39.7 %copy-start.1 = (f32[16,2048]{1,0:T(8,128)S(1)}, f32[16,2048]{1,0:T(8,128)}, u32[]{:S(2)}) copy-start(f32[16,2048]{1,0:T(8,128)} %m_ref.1) | copy-start | bytes 393220
  0.7 39.7 %copy-start.2 = (f32[16,2048]{1,0:T(8,128)S(1)}, f32[16,2048]{1,0:T(8,128)}, u32[]{:S(2)}) copy-start(f32[16,2048]{1,0:T(8,128)} %s_ref.1) | copy-start | bytes 393220
